TPU v7x, 32 devices: a whole 2x2x4 slice. The times are simulated.
32 devices in a mesh: grp: 2 (over y), par: 8 (over z, x), ex: 2 (over core).
Axes of the slice: x: 2, y: 2, z: 4, core: 2. Of those that a mesh axis runs over, the one named last changes fastest.
Arguments:
- hidden: bfloat16 [4, 256, 8192], P(('grp', 'ex'), None, 'par'), parts along dimension 0, may hold values from -6 to 6
- cotangent: bfloat16 [4, 256, 5120], P(('grp', 'ex')), parts along dimension 0, may hold values from -0.3984375 to 0.3984375
- signs: int32 [8192, 320], P('par'), may hold values from 0 to 65535
Outputs:
- projected: float32 [4, 8192, 8192], P(('grp', 'ex'), 'par'), parts along dimension 0
There are 2 independent parts, one for each index of `grp`. A program takes and returns all parts, laid end to end along the dimension named above; an argument that names none is the same for every part. Nothing has to cross between parts.
All inputs are finite; a program needn't handle non-finite values.
Results may differ from a plain program's by a relative error of at most 0.0003.
Values sent between devices are 32-bit elements; how exact they have to be, the bound alone decides.
A program may use at most 256 MiB of HBM per device.

v0:
```python
import math

import jax
import jax.numpy as jnp
from jax import lax
from jax.sharding import PartitionSpec as P

FFW = 8192
DP = 8192


def unpack_signs(signs):
    shifts = jnp.arange(16, dtype=jnp.int32)
    bits = signs[:, :, None] >> shifts[None, None, :] & 1
    return (1 - 2 * bits).reshape(signs.shape[0], -1).astype(jnp.float32)


def parity_sign(masked, width):
    parity = jnp.zeros(masked.shape, jnp.int32)
    for place in range(width):
        parity = parity ^ masked >> place & 1
    return (1 - 2 * parity).astype(jnp.float32)


def walsh_table(order):
    indices = jnp.arange(order, dtype=jnp.int32)
    return parity_sign(indices[:, None] & indices[None, :], max(order.bit_length(), 1))


def walsh_axis(values, axis):
    length = values.shape[axis]
    power = length.bit_length() - 1
    low_size = 2 ** ((power + 1) // 2)
    high_size = length // low_size
    leading = math.prod(values.shape[:axis])
    trailing = math.prod(values.shape[axis + 1 :])
    blocks = values.reshape(leading, high_size, low_size, trailing)
    blocks = jnp.einsum(
        "pabq,bc->pacq", blocks, walsh_table(low_size), precision=lax.Precision.HIGHEST
    )
    blocks = jnp.einsum(
        "pacq,ad->pdcq", blocks, walsh_table(high_size), precision=lax.Precision.HIGHEST
    )
    return blocks.reshape(values.shape)


def body(hidden, cotangent, signs):
    gradient = jnp.einsum("etr,etd->erd", hidden, cotangent, preferred_element_type=jnp.float32)
    sign_table = unpack_signs(signs)
    padded = jnp.pad(gradient * sign_table[None], ((0, 0), (0, 0), (0, DP - gradient.shape[2])))
    columns_done = walsh_axis(padded, 2)
    rows_done = walsh_axis(
        lax.all_to_all(columns_done, "par", split_axis=2, concat_axis=1, tiled=True), 1
    )
    result = lax.all_to_all(rows_done, "par", split_axis=1, concat_axis=2, tiled=True)
    return result * (1.0 / math.sqrt(FFW * DP))


def solution(mesh):
    in_specs = (P(("grp", "ex"), None, "par"), P(("grp", "ex"), None, None), P("par", None))
    out_specs = P(("grp", "ex"), "par", None)
    return jax.shard_map(body, mesh=mesh, in_specs=in_specs, out_specs=out_specs, check_vma=False)
```

profile of v0, /device:TPU:0, one launch (start us, length us, event | category | flops | bytes accessed | tf_op | source)
XLA Modules:
  0.0 2086.2 jit_solution(14607529731374799901)
XLA Ops:
  0.0 0.0 copy-start
  0.0 0.1 shift_right_arithmetic.128
  0.1 11.8 shift_right_arithmetic.125
  12.0 19.9 copy.23
  31.9 0.0 copy-done
  31.9 0.0 copy-done.2
  31.9 13.9 multiply_bitcast_fusion
  45.7 10.2 pad_bitcast_fusion
  56.0 12.4 copy.34
  68.4 58.6 %fusion.4 = f32[1024,64,128]{0,2,1:T(8,128)} fusion(f32[1024,64,128]{2,1,0:T(8,128)} %bitcast.54), kind=kOutput, calls=%fused_computation.8 | convolution fusion | flops 12885344256 | bytes 67108864 | tf_op jit(solution)/shard_map/pabq,bc->pacq/dot_general | solution.py:38
  127.0 32.1 %copy.25 = f32[1024,64,128]{2,1,0:T(8,128)} copy(f32[1024,64,128]{0,2,1:T(8,128)} %fusion.4) | data formatting | bytes 67108864 | tf_op jit(solution)/shard_map/reshape.9
  159.1 36.5 %convolution_bitcast_fusion = f32[1024,64,128,1]{2,1,0,3:T(8,128)} fusion(f32[1024,64,128]{2,1,0:T(8,128)} %copy.25), kind=kOutput, calls=%fused_computation.7 | convolution fusion | flops 6442549248 | bytes 67108864 | tf_op jit(solution)/shard_map/pacq,ad->pdcq/dot_general | solution.py:41
  195.6 35.9 %reshape.57 = f32[1,1024,8192]{2,1,0:T(8,128)} reshape(f32[1024,64,128,1]{2,1,0,3:T(8,128)} %convolution_bitcast_fusion) | data formatting | bytes 67108864 | tf_op jit(solution)/shard_map/reshape | solution.py:44
  231.5 68.5 %copy.26 = f32[1,1024,8192]{1,0,2:T(1,128)} copy(f32[1,1024,8192]{2,1,0:T(8,128)} %reshape.57) | data formatting | bytes 67108864 | tf_op jit(solution)/shard_map/reshape | solution.py:44
  299.9 735.1 %all_to_all.24 = f32[1,1024,8192]{1,0,2:T(1,128)} all-to-all(f32[1,1024,8192]{1,0,2:T(1,128)} %copy.26), channel_id=1, replica_groups=mesh['grp'=2,'par'=8,'ex'=2] {'par'}, dimensions={2} | all-to-all | bytes 67108864 | tf_op jit(solution)/shard_map/all_to_all | solution.py:53
  1035.1 78.2 %copy.27 = f32[1,1024,8,1024]{3,1,2,0:T(8,128)} copy(f32[1,1024,8,1024]{1,0,3,2:T(1,128)} %bitcast.55) | data formatting | bytes 67108864 | tf_op jit(solution)/shard_map/all_to_all | solution.py:53
  1113.3 36.9 %convolution_bitcast_fusion.1 = f32[64,128,1024]{2,1,0:T(8,128)} fusion(f32[64,128,1024]{2,1,0:T(8,128)} %bitcast.56), kind=kOutput, calls=%fused_computation.9 | convolution fusion | flops 12885344256 | bytes 67108864 | tf_op jit(solution)/shard_map/pabq,bc->pacq/dot_general | solution.py:38
  1150.2 59.6 %fusion = f32[64,128,1024]{2,0,1:T(8,128)} fusion(f32[64,128,1024]{2,1,0:T(8,128)} %convolution_bitcast_fusion.1), kind=kOutput, calls=%fused_computation.1 | convolution fusion | flops 6442549248 | bytes 67108864 | tf_op jit(solution)/shard_map/pacq,ad->pdcq/dot_general | solution.py:41
  1209.8 31.8 %copy.29 = f32[64,128,1024]{2,1,0:T(8,128)} copy(f32[64,128,1024]{2,0,1:T(8,128)} %fusion) | data formatting | bytes 67108864 | tf_op jit(solution)/shard_map/pacq,ad->pdcq/dot_general | solution.py:41
  1241.6 37.9 %copy.30 = f32[1,8192,1024]{2,0,1:T(1,128)} copy(f32[1,8192,1024]{2,1,0:T(8,128)} %bitcast.57) | data formatting | bytes 67108864 | tf_op jit(solution)/shard_map/reshape;pacq,ad->pdcq/transpose | solution.py:44
  1279.5 728.4 %all_to_all.25 = f32[1,8192,1024]{2,0,1:T(1,128)S(1)} all-to-all(f32[1,8192,1024]{2,0,1:T(1,128)} %copy.30), channel_id=1, replica_groups=mesh['grp'=2,'par'=8,'ex'=2] {'par'}, dimensions={1} | all-to-all | bytes 67108864 | tf_op jit(solution)/shard_map/all_to_all | solution.py:55
  2007.9 15.0 copy_multiply_fusion
  2022.8 31.9 %copy.32 = f32[1,1024,8,1024]{1,3,2,0:T(8,128)} copy(f32[1,1024,8,1024]{3,1,2,0:T(8,128)} %bitcast.58) | data formatting | bytes 67108864 | tf_op jit(solution)/shard_map/mul | solution.py:56
  2054.7 31.2 %copy.33 = f32[1,1024,8192]{2,1,0:T(8,128)} copy(f32[1,1024,8192]{1,2,0:T(8,128)} %bitcast.59) | data formatting | bytes 67108864 | tf_op jit(solution)/shard_map/mul | solution.py:56
  (4 shorter events, 0.0 us)
Async XLA Ops:
  0.0 31.9 %copy-start = (bf16[1,256,5120]{2,1,0:T(8,128)(2,1)S(1)}, bf16[1,256,5120]{2,1,0:T(8,128)(2,1)}, u32[]{:S(2)}) copy-start(bf16[1,256,5120]{2,1,0:T(8,128)(2,1)} %param.4) | copy-start | bytes 7864324
  0.0 31.9 %copy-start.2 = (bf16[1,256,1024]{2,1,0:T(8,128)(2,1)S(1)}, bf16[1,256,1024]{2,1,0:T(8,128)(2,1)}, u32[]{:S(2)}) copy-start(bf16[1,256,1024]{2,1,0:T(8,128)(2,1)} %param.3) | copy-start | bytes 1572868
  2054.7 31.2 %copy-start.1 = (bf16[1,256,5120]{2,1,0:T(8,128)(2,1)S(1)}, bf16[1,256,5120]{2,1,0:T(8,128)(2,1)}, u32[]{:S(2)}) copy-start(bf16[1,256,5120]{2,1,0:T(8,128)(2,1)} %param.4) | copy-start | bytes 7864324
where the time goes:
time: 2100 us; the launch traced here: 2090 us
  blocking collectives  1460 us (70%)
  local copies, waits for them, and re-layouts  402 us (19%)
  matrix products  206 us (10%)
    all_to_all x1, blocking collectives, body(): lax.all_to_all(columns_done, 'par', split_axis=2, concat_axis=1, tiled=True)  735 us
    all_to_all x1, blocking collectives, body(): lax.all_to_all(rows_done, 'par', split_axis=1, concat_axis=2, tiled=True)  728 us
    reshape x2, local copies, waits for them, and re-layouts, walsh_axis(): return blocks.reshape(values.shape)  104 us
    dot_general x2, matrix products, walsh_axis(): jnp.einsum('pacq,ad->pdcq', blocks, walsh_table(high_size), precision=lax...  96.1 us
    dot_general x2, matrix products, walsh_axis(): jnp.einsum('pabq,bc->pacq', blocks, walsh_table(low_size), precision=lax....  95.6 us
    all_to_all x1, local copies, waits for them, and re-layouts, body(): lax.all_to_all(columns_done, 'par', split_axis=2, concat_axis=1, tiled=True)  78.2 us
    mul x2, local copies, waits for them, and re-layouts, body(): return result * (1.0 / math.sqrt(FFW * DP))  63.1 us

commit v1 on v0

v1 whole, which is shorter than its diff:
```python
import functools
import math

import jax
import jax.numpy as jnp
import numpy as np
from jax import lax
from jax.experimental import pallas as pl
from jax.experimental.pallas import tpu as pltpu
from jax.sharding import PartitionSpec as P

DP = 8192
CB = 256
OUT_ROWS = 64


def walsh_np(order):
    idx = np.arange(order)
    both = idx[:, None] & idx[None, :]
    parity = np.zeros_like(both)
    for place in range(order.bit_length()):
        parity ^= (both >> place) & 1
    return (1 - 2 * parity).astype(np.float32)


def split(x):
    hi = x.astype(jnp.bfloat16)
    return hi, (x - hi.astype(jnp.float32)).astype(jnp.bfloat16)


def butterflies(parts):
    parts = list(parts)
    half = 1
    while half < len(parts):
        for start in range(0, len(parts), 2 * half):
            for k in range(start, start + half):
                a, b = parts[k], parts[k + half]
                if b is None:
                    parts[k + half] = a
                else:
                    parts[k], parts[k + half] = a + b, a - b
        half *= 2
    return parts


def pair_sign(p, q, n):
    parity = jnp.int32(0)
    for place in range(n.bit_length()):
        parity = parity ^ (((p & q) >> place) & 1)
    return (1 - 2 * parity).astype(jnp.float32)


def kernel(n, me_ref, hid_ref, sgn_ref, cot_ref, hc_ref, hr_ref, out_ref, hb, y, z):
    step = pl.program_id(0)
    toks, rows = hb.shape
    blocks = z.shape[0]
    ft = min(256, rows)
    mask = jnp.left_shift(jnp.int32(1), lax.broadcasted_iota(jnp.int32, (16, ft), 0))

    @pl.when(step == 0)
    def _():
        y[...] = jnp.zeros_like(y)

    @pl.when(step < n)
    def _():
        hb[...] = (hid_ref[0] * pair_sign(me_ref[0], step, n)).astype(jnp.bfloat16)

        def chunk(ci, carry):
            c = cot_ref[pl.ds(pl.multiple_of(ci * CB, CB), CB), :]
            for f in range(0, rows, ft):
                g = jnp.dot(c, hb[:, f : f + ft], preferred_element_type=jnp.float32)
                for w in range(CB // 16):
                    word = sgn_ref[0, pl.ds(ci * (CB // 16) + w, 1), f : f + ft]
                    bit = (word & mask) != 0
                    gw = g[16 * w : 16 * w + 16]
                    at = pl.ds(pl.multiple_of(ci * CB + 16 * w, 16), 16)
                    old = y[at, f : f + ft]
                    y[at, f : f + ft] = jnp.where(bit, old - gw, old + gw)
            return carry

        lax.fori_loop(0, blocks, chunk, 0)

    @pl.when((step >= n) & (step < n + blocks))
    def _():
        b = step - n
        hi, lo = split(y[pl.ds(pl.multiple_of(b * CB, CB), CB), :])
        hc = hc_ref[...]
        t = jnp.dot(hc, hi, preferred_element_type=jnp.float32) + jnp.dot(
            hc, lo, preferred_element_type=jnp.float32
        )
        groups = butterflies([t[:, f : f + ft] for f in range(0, rows, ft)])
        hr = hr_ref[...]
        dims = (((1,), (1,)), ((), ()))
        for a, group in enumerate(groups):
            hi, lo = split(group)
            z[b, a * ft : (a + 1) * ft, :] = lax.dot_general(
                hr, hi, dims, preferred_element_type=jnp.float32
            ) + lax.dot_general(hr, lo, dims, preferred_element_type=jnp.float32)

    @pl.when(step >= n + blocks)
    def _():
        first = (step - n - blocks) * OUT_ROWS

        def strip(r, carry):
            rr = pl.multiple_of(first + r * 8, 8)
            ro = pl.multiple_of(r * 8, 8)
            for l in range(0, CB, 128):
                parts = [z[b, pl.ds(rr, 8), l : l + 128] for b in range(blocks)]
                parts = butterflies(parts + [None] * (DP // CB - blocks))
                for b, part in enumerate(parts):
                    out_ref[pl.ds(ro, 8), b * CB + l : b * CB + l + 128] = part
            return carry

        lax.fori_loop(0, OUT_ROWS // 8, strip, 0)


def transform(n, me, hid, sgn, cot_t):
    toks, rows = hid.shape[1:]
    width = cot_t.shape[0]
    blocks = width // CB
    words = sgn.shape[1]
    ft = min(256, rows)
    hc = jnp.asarray(walsh_np(CB), jnp.bfloat16)
    scale = 1.0 / math.sqrt(n * rows * DP)
    hr = jnp.asarray(walsh_np(ft) * scale, jnp.bfloat16)
    tiles = rows // OUT_ROWS
    whole = lambda s: (0, 0)
    return pl.pallas_call(
        functools.partial(kernel, n),
        grid=(n + blocks + tiles,),
        out_shape=jax.ShapeDtypeStruct((rows, DP), jnp.float32),
        in_specs=[
            pl.BlockSpec(memory_space=pltpu.SMEM),
            pl.BlockSpec((1, toks, rows), lambda s: (jnp.minimum(s, n - 1), 0, 0)),
            pl.BlockSpec((1, words, rows), lambda s: (jnp.minimum(s, n - 1), 0, 0)),
            pl.BlockSpec((width, toks), whole, pipeline_mode=pl.Buffered(1)),
            pl.BlockSpec((CB, CB), whole),
            pl.BlockSpec((ft, ft), whole),
        ],
        out_specs=pl.BlockSpec((OUT_ROWS, DP), lambda s: (jnp.maximum(s - n - blocks, 0), 0)),
        scratch_shapes=[
            pltpu.VMEM((toks, rows), jnp.bfloat16),
            pltpu.VMEM((width, rows), jnp.float32),
            pltpu.VMEM((blocks, rows, CB), jnp.float32),
        ],
        compiler_params=pltpu.CompilerParams(vmem_limit_bytes=60 * 1024 * 1024),
    )(me, hid, sgn, cot_t, hc, hr)


def body(n, hidden, cotangent, signs):
    me = lax.axis_index("par").astype(jnp.int32).reshape(1)
    ex = lax.axis_index("ex")
    words = signs.shape[1]
    half = words // 2
    signs_t = lax.dynamic_slice_in_dim(signs, ex * half, half, axis=1).T
    sgn = lax.all_gather(signs_t, ("par", "ex")).reshape(n, words, signs.shape[0])
    hid = lax.all_gather(hidden[0].astype(jnp.float32), "par")
    return transform(n, me, hid, sgn, cotangent[0].T)[None]


def solution(mesh):
    in_specs = (P(("grp", "ex"), None, "par"), P(("grp", "ex"), None, None), P("par", None))
    out_specs = P(("grp", "ex"), "par", None)
    return jax.shard_map(
        functools.partial(body, mesh.shape["par"]),
        mesh=mesh,
        in_specs=in_specs,
        out_specs=out_specs,
        check_vma=False,
    )
```

time: 2100 us -> 354 us (0.17)
  blocking collectives: 1460 us -> 0 us
  local copies, waits for them, and re-layouts: 402 us -> 5.34 us
  waiting for transfers between devices: 0 us -> 211 us
  matrix products: 206 us -> 0 us
  Pallas kernels: 0 us -> 122 us
    all_to_all x2 -> x0, blocking collectives: 1460 us -> none  [the longest x1 735 us: body(): lax.all_to_all(columns_done, 'par', split_axis=2, concat_axis=1, tiled=True)]
    all_gather x0 -> x2, waiting for transfers between devices: none -> 211 us  [the longest x1 123 us: body(): hid = lax.all_gather(hidden[0].astype(jnp.float32), 'par')]
    dot_general x5 -> x0, matrix products: 206 us -> none  [the longest x2 96.1 us: walsh_axis(): jnp.einsum('pacq,ad->pdcq', blocks, walsh_table(high_size), precision=lax...]
    pallas_call x0 -> x1, Pallas kernels: none -> 122 us  [transform(): pl.pallas_call(functools.partial(kernel, n), grid=(n + blocks + tiles,),...]
    reshape x2 -> x0, local copies, waits for them, and re-layouts: 104 us -> none  [walsh_axis(): return blocks.reshape(values.shape)]
    all_to_all x1 -> x0, local copies, waits for them, and re-layouts: 78.2 us -> none  [body(): lax.all_to_all(columns_done, 'par', split_axis=2, concat_axis=1, tiled=True)]
    mul x2 -> x0, local copies, waits for them, and re-layouts: 63.1 us -> none  [body(): return result * (1.0 / math.sqrt(FFW * DP))]
    transpose x1, local copies, waits for them, and re-layouts: 37.9 us -> 0.93 us  [body(): signs_t = lax.dynamic_slice_in_dim(signs, ex * half, half, axis=1).T]
  transfers between devices with their start and end apart: 0 -> 2, of which waited for: 0 -> 2; matrix products, arithmetic and copies ran while one was open for 0% -> 2% of each run, Pallas kernels for 0% -> 0%
where the time goes in v1:
time: 354 us
  waiting for transfers between devices  211 us (60%)
  Pallas kernels  122 us (34%)
  between operations  13.4 us (4%)
  local copies, waits for them, and re-layouts  5.34 us (2%)
    all_gather x1, waiting for transfers between devices, body(): hid = lax.all_gather(hidden[0].astype(jnp.float32), 'par')  123 us
    pallas_call x1, Pallas kernels, transform(): pl.pallas_call(functools.partial(kernel, n), grid=(n + blocks + tiles,),...  122 us
    all_gather x1, waiting for transfers between devices, body(): lax.all_gather(signs_t, ('par', 'ex')).reshape(n, words, signs.shape[0])  88.4 us
  transfers between devices with their start and end apart: 2, of which 2 were waited for; matrix products, arithmetic and copies ran while one was open for 2% of the time, Pallas kernels for 0%

profile of v1, /device:TPU:0, one launch (start us, length us, event | category | flops | bytes accessed | tf_op | source)
XLA Modules:
  0.0 353.9 jit_solution(5392525862068584106)
XLA Ops:
  6.5 0.0 copy-start
  6.5 0.0 all-gather.4.cloned.1.call-start
  6.5 2.2 convert_element_type.4
  8.8 0.0 all-gather.4.cloned.1.call-update
  8.8 0.0 all-gather.6.cloned.1.call-start
  8.8 0.0 copy-done
  8.9 0.9 dynamic-slice_bitcast_fusion
  9.8 0.0 all-gather.6.cloned.1.call-update
  9.8 4.4 %copy.7 = bf16[1,256,5120]{1,2,0:T(8,128)(2,1)} copy(bf16[1,256,5120]{2,1,0:T(8,128)(2,1)} %param.6) | data formatting | bytes 5242880 | tf_op args[1]
  14.2 122.9 %all-gather.4.cloned.1.call-done.hid_ref = f32[8,256,1024]{2,1,0:T(8,128)} async-done(((f32[1,256,1024]{2,1,0:T(8,128)}), f32[8,256,1024]{2,1,0:T(8,128)}) %all-gather.4.cloned.1.call-update) | async-done | bytes 8388624 | tf_op jit(solution)/shard_map/all_gather | solution.py:157
  137.1 88.4 %all-gather.6.cloned.1.call-done = s32[2560,1024]{1,0:T(8,128)} async-done(((s32[160,1024]{1,0:T(8,128)}), s32[2560,1024]{1,0:T(8,128)}) %all-gather.6.cloned.1.call-update) | async-done | bytes 10485776 | tf_op jit(solution)/shard_map/all_gather | solution.py:156
  225.5 121.6 %shard_map.55 = f32[1024,8192]{1,0:T(8,128)} custom-call(s32[1]{0:T(128)} %bitcast.me_ref, f32[8,256,1024]{2,1,0:T(8,128)} %all-gather.4.cloned.1.call-done.hid_ref, s32[8,320,1024]{2,1,0:T(8,128)} %bitcast.9, bf16[5120,256]{1,0:T(8,128)(2,1)} %bitcast.8, bf16[256,256]{1,0:T(8,128)(2,1)} %constant.18.clone.hc_ref, bf16[256,256]{1,0:T(8,128)(2,1)} %constant.19.clone.hr_ref), custom_call_target="tpu_custom_call" | custom-call | tf_op jit(solution)/shard_map/pallas_call | solution.py:128
Async XLA Ops:
  6.5 2.3 copy-start
  6.5 130.6 %all-gather.4.cloned.1.call-start = ((), (), s32[]{:S(2)}) async-start(), calls=%async_computation | async-start | bytes 9437184 | tf_op jit(solution)/shard_map/all_gather | solution.py:157
  8.8 216.7 %all-gather.6.cloned.1.call-start = ((), (), s32[]{:S(2)}) async-start(), calls=%async_computation.1 | async-start | bytes 11141120 | tf_op jit(solution)/shard_map/all_gather | solution.py:156
Sparse Core Ops, SparseCore 0:
  9.5 127.6 all-gather.3
  139.4 86.0 all-gather.5

commit v2 on v1

v2 whole, which is shorter than its diff:
```python
import functools
import math

import jax
import jax.numpy as jnp
import numpy as np
from jax import lax
from jax.experimental import pallas as pl
from jax.experimental.pallas import tpu as pltpu
from jax.sharding import PartitionSpec as P

DP = 8192
CB = 256
OUT_ROWS = 64


def walsh_np(order):
    idx = np.arange(order)
    both = idx[:, None] & idx[None, :]
    parity = np.zeros_like(both)
    for place in range(order.bit_length()):
        parity ^= (both >> place) & 1
    return (1 - 2 * parity).astype(np.float32)


def split(x):
    hi = x.astype(jnp.bfloat16)
    return hi, (x - hi.astype(jnp.float32)).astype(jnp.bfloat16)


def butterflies(parts):
    parts = list(parts)
    half = 1
    while half < len(parts):
        for start in range(0, len(parts), 2 * half):
            for k in range(start, start + half):
                a, b = parts[k], parts[k + half]
                if b is None:
                    parts[k + half] = a
                else:
                    parts[k], parts[k + half] = a + b, a - b
        half *= 2
    return parts


def pair_sign(p, q, n):
    parity = jnp.int32(0)
    for place in range(n.bit_length()):
        parity = parity ^ (((p & q) >> place) & 1)
    return (1 - 2 * parity).astype(jnp.float32)


def ring_place(p, n):
    return jnp.where(p % 2 == 0, p // 2, n - 1 - p // 2)


def ring_index(k, n):
    return jnp.where(k < n // 2, 2 * k, 2 * (n - 1 - k) + 1)


def gather_kernel(
    n, hid_ref, sgn_ref, cot_ref, y_out, hid, sgn, hb, y,
    hid_send, hid_recv, sgn_send, sgn_recv, mate_send, mate_recv, out_sem,
):
    toks, rows = hb.shape
    blocks = y.shape[0] // CB
    words = sgn.shape[2]
    far = n // 2
    ft = min(256, rows)
    me = lax.axis_index("par")
    core = lax.axis_index("ex")
    place = ring_place(me, n)
    left = ring_index((place + n - 1) % n, n)
    right = ring_index((place + 1) % n, n)
    ahead = (right, left)
    mesh_id = pl.DeviceIdType.MESH

    barrier = pltpu.get_barrier_semaphore()
    for target in ({"par": left}, {"par": right}, {"ex": 1 - core}):
        pl.semaphore_signal(barrier, inc=1, device_id=target, device_id_type=mesh_id)
    pl.semaphore_wait(barrier, 3)

    def slot(side, d):
        if d == 0:
            return 0
        return n - 1 if d == far else 1 + 2 * (d - 1) + side

    def part(side, d, size):
        return pl.ds(side * (size // 2), size // 2) if d == far else pl.ds(0, size)

    def send_hid(side, d):
        at = part(side, d, toks)
        src = hid_ref.at[at] if d == 1 else hid.at[slot(side, d - 1), at]
        return pltpu.make_async_remote_copy(
            src_ref=src,
            dst_ref=hid.at[slot(side, d), at],
            send_sem=hid_send.at[side, d],
            recv_sem=hid_recv.at[side, d],
            device_id={"par": ahead[side]},
            device_id_type=mesh_id,
        )

    def send_sgn(side, d):
        at = part(side, d, words)
        src = sgn_ref.at[at] if d == 1 else sgn.at[slot(side, d - 1), core, at]
        return pltpu.make_async_remote_copy(
            src_ref=src,
            dst_ref=sgn.at[slot(side, d), core, at],
            send_sem=sgn_send.at[side, d],
            recv_sem=sgn_recv.at[side, d],
            device_id={"par": ahead[side]},
            device_id_type=mesh_id,
        )

    def send_mate(s):
        return pltpu.make_async_remote_copy(
            src_ref=sgn_ref if s == 0 else sgn.at[s, core],
            dst_ref=sgn.at[s, core],
            send_sem=mate_send.at[s],
            recv_sem=mate_recv.at[s],
            device_id={"ex": 1 - core},
            device_id_type=mesh_id,
        )

    mate_copies = [send_mate(s) for s in range(n)]

    def wait_mate(s):
        pltpu.make_async_remote_copy(
            src_ref=sgn.at[s, 1 - core],
            dst_ref=sgn.at[s, 1 - core],
            send_sem=mate_send.at[s],
            recv_sem=mate_recv.at[s],
            device_id={"ex": 1 - core},
            device_id_type=mesh_id,
        ).wait_recv()

    def store_block(ci):
        at = pl.ds(pl.multiple_of(ci * CB, CB), CB)
        return pltpu.make_async_copy(y.at[at], y_out.at[at], out_sem.at[ci])

    mask = jnp.left_shift(jnp.int32(1), lax.broadcasted_iota(jnp.int32, (16, ft), 0))
    per_block = CB // 16

    def accumulate(block, s, q, first=False, last=False):
        hb[...] = (block[...] * pair_sign(me, q, n)).astype(jnp.bfloat16)

        for h in range(2):

            def chunk(ci, carry):
                row = ci - h * (blocks // 2)
                c = cot_ref[pl.ds(pl.multiple_of(ci * CB, CB), CB), :]
                for f in range(0, rows, ft):
                    g = jnp.dot(c, hb[:, f : f + ft], preferred_element_type=jnp.float32)
                    for w in range(per_block):
                        word = sgn[s, h, pl.ds(row * per_block + w, 1), f : f + ft]
                        bit = (word & mask) != 0
                        gw = g[16 * w : 16 * w + 16]
                        at = pl.ds(pl.multiple_of(ci * CB + 16 * w, 16), 16)
                        if first:
                            y[at, f : f + ft] = jnp.where(bit, -gw, gw)
                        else:
                            old = y[at, f : f + ft]
                            y[at, f : f + ft] = jnp.where(bit, old - gw, old + gw)
                if last:
                    store_block(ci).start()
                return carry

            lax.fori_loop(h * (blocks // 2), (h + 1) * (blocks // 2), chunk, 0)

    started = []

    def go(copy):
        copy.start()
        started.append(copy)

    for side in range(2):
        go(send_sgn(side, 1))
    for side in range(2):
        go(send_hid(side, 1))
    go(mate_copies[0])
    own = pltpu.make_async_copy(sgn_ref, sgn.at[0, core], out_sem.at[0])
    own.start()
    own.wait()
    wait_mate(0)
    accumulate(hid_ref, 0, me, first=True)

    for d in range(1, far + 1):
        for side in range(2):
            send_sgn(side, d).wait_recv()
            if d < far:
                go(send_sgn(side, d + 1))
                go(mate_copies[slot(side, d)])
        if d == far:
            go(mate_copies[n - 1])
        for side in range(2):
            send_hid(side, d).wait_recv()
            if d < far:
                go(send_hid(side, d + 1))
        if d < far:
            for side in range(2):
                s = slot(side, d)
                wait_mate(s)
                k = (place + (n - d if side == 0 else d)) % n
                accumulate(hid.at[s], s, ring_index(k, n))
        else:
            wait_mate(n - 1)
            accumulate(hid.at[n - 1], n - 1, ring_index((place + far) % n, n), last=True)

    for copy in started:
        copy.wait_send()
    for ci in range(blocks):
        store_block(ci).wait()


def gathered_gradient(n, hid, sgn, cot_t):
    toks, rows = hid.shape
    width = cot_t.shape[0]
    half = sgn.shape[0]
    far = n // 2
    vmem = pl.BlockSpec(memory_space=pltpu.VMEM)
    dma = pltpu.SemaphoreType.DMA
    return pl.pallas_call(
        functools.partial(gather_kernel, n),
        out_shape=jax.ShapeDtypeStruct((width, rows), jnp.float32),
        in_specs=[vmem, vmem, vmem],
        out_specs=pl.BlockSpec(memory_space=pl.ANY),
        scratch_shapes=[
            pltpu.VMEM((n, toks, rows), jnp.float32),
            pltpu.VMEM((n, 2, half, rows), jnp.int32),
            pltpu.VMEM((toks, rows), jnp.bfloat16),
            pltpu.VMEM((width, rows), jnp.float32),
            dma((2, far + 1)),
            dma((2, far + 1)),
            dma((2, far + 1)),
            dma((2, far + 1)),
            dma((n,)),
            dma((n,)),
            dma((width // CB,)),
        ],
        compiler_params=pltpu.CompilerParams(
            collective_id=0, has_side_effects=True, vmem_limit_bytes=60 * 1024 * 1024
        ),
    )(hid, sgn, cot_t)


def transform_kernel(y_ref, hc_ref, hr_ref, out_ref, z):
    step = pl.program_id(0)
    blocks, rows = z.shape[:2]
    ft = min(256, rows)

    @pl.when(step < blocks)
    def _():
        hi, lo = split(y_ref[...])
        hc = hc_ref[...]
        t = jnp.dot(hc, hi, preferred_element_type=jnp.float32) + jnp.dot(
            hc, lo, preferred_element_type=jnp.float32
        )
        groups = butterflies([t[:, f : f + ft] for f in range(0, rows, ft)])
        hr = hr_ref[...]
        dims = (((1,), (1,)), ((), ()))
        for a, group in enumerate(groups):
            hi, lo = split(group)
            z[step, a * ft : (a + 1) * ft, :] = lax.dot_general(
                hr, hi, dims, preferred_element_type=jnp.float32
            ) + lax.dot_general(hr, lo, dims, preferred_element_type=jnp.float32)

    @pl.when(step >= blocks)
    def _():
        first = (step - blocks) * OUT_ROWS

        def strip(r, carry):
            rr = pl.multiple_of(first + r * 8, 8)
            ro = pl.multiple_of(r * 8, 8)
            for l in range(0, CB, 128):
                parts = [z[b, pl.ds(rr, 8), l : l + 128] for b in range(blocks)]
                parts = butterflies(parts + [None] * (DP // CB - blocks))
                for b, part in enumerate(parts):
                    out_ref[pl.ds(ro, 8), b * CB + l : b * CB + l + 128] = part
            return carry

        lax.fori_loop(0, OUT_ROWS // 8, strip, 0)


def transform(n, y):
    width, rows = y.shape
    blocks = width // CB
    ft = min(256, rows)
    hc = jnp.asarray(walsh_np(CB), jnp.bfloat16)
    scale = 1.0 / math.sqrt(n * rows * DP)
    hr = jnp.asarray(walsh_np(ft) * scale, jnp.bfloat16)
    whole = lambda s: (0, 0)
    return pl.pallas_call(
        transform_kernel,
        grid=(blocks + rows // OUT_ROWS,),
        out_shape=jax.ShapeDtypeStruct((rows, DP), jnp.float32),
        in_specs=[
            pl.BlockSpec((CB, rows), lambda s: (jnp.minimum(s, blocks - 1), 0)),
            pl.BlockSpec((CB, CB), whole),
            pl.BlockSpec((ft, ft), whole),
        ],
        out_specs=pl.BlockSpec((OUT_ROWS, DP), lambda s: (jnp.maximum(s - blocks, 0), 0)),
        scratch_shapes=[pltpu.VMEM((blocks, rows, CB), jnp.float32)],
        compiler_params=pltpu.CompilerParams(vmem_limit_bytes=60 * 1024 * 1024),
    )(y, hc, hr)


def body(n, hidden, cotangent, signs):
    half = signs.shape[1] // 2
    sgn = lax.dynamic_slice_in_dim(signs, lax.axis_index("ex") * half, half, axis=1).T
    y = gathered_gradient(n, hidden[0].astype(jnp.float32), sgn, cotangent[0].T)
    return transform(n, y)[None]


def solution(mesh):
    in_specs = (P(("grp", "ex"), None, "par"), P(("grp", "ex"), None, None), P("par", None))
    out_specs = P(("grp", "ex"), "par", None)
    return jax.shard_map(
        functools.partial(body, mesh.shape["par"]),
        mesh=mesh,
        in_specs=in_specs,
        out_specs=out_specs,
        check_vma=False,
    )
```

time: 354 us -> 199 us (0.56)
  waiting for transfers between devices: 211 us -> 0 us
  Pallas kernels: 122 us -> 188 us
  between operations: 13.4 us -> 0.01 us
    all_gather x2 -> x0, waiting for transfers between devices: 211 us -> none  [the longest x1 123 us: body(): hid = lax.all_gather(hidden[0].astype(jnp.float32), 'par')]
    pallas_call x1 -> x2, Pallas kernels: 122 us -> 188 us  [the longest x1 150 us: gathered_gradient(): pl.pallas_call(functools.partial(gather_kernel, n), out_shape=jax.ShapeDt...]
  transfers between devices with their start and end apart: 2 -> 0, of which waited for: 2 -> 0; matrix products, arithmetic and copies ran while one was open for 2% -> 0% of each run, Pallas kernels for 0% -> 0%
where the time goes in v2:
time: 199 us; the launch traced here: 196 us
  Pallas kernels  188 us (94%)
  local copies, waits for them, and re-layouts  6.61 us (3%)
  other arithmetic  2.13 us (1%)
    pallas_call x1, Pallas kernels, gathered_gradient(): pl.pallas_call(functools.partial(gather_kernel, n), out_shape=jax.ShapeDt...  150 us
    pallas_call x1, Pallas kernels, transform(): pl.pallas_call(transform_kernel, grid=(blocks + rows // OUT_ROWS,), out_s...  37.4 us
    unnamed x3, local copies, waits for them, and re-layouts  5.69 us

profile of v2, /device:TPU:0, one launch (start us, length us, event | category | flops | bytes accessed | tf_op | source)
XLA Modules:
  0.0 196.3 jit_solution(14829489785758497990)
XLA Ops:
  0.0 0.0 copy-start
  0.0 1.3 copy-done
  1.3 0.9 dynamic-slice_bitcast_fusion.sgn_ref
  2.2 2.1 %bitcast_convert_fusion.hid_ref = f32[256,1024]{1,0:T(8,128)} fusion(bf16[1,256,1024]{2,1,0:T(8,128)(2,1)} %param.5), kind=kLoop, calls=%fused_computation.1 | loop fusion | flops 262144 | bytes 1572864 | tf_op jit(solution)/shard_map/convert_element_type | solution.py:310
  4.4 4.4 %copy.6 = bf16[1,256,5120]{1,2,0:T(8,128)(2,1)} copy(bf16[1,256,5120]{2,1,0:T(8,128)(2,1)} %param.6) | data formatting | bytes 5242880 | tf_op args[1]
  8.7 150.1 %shard_map.55.y_ref = f32[5120,1024]{1,0:T(8,128)} custom-call(f32[256,1024]{1,0:T(8,128)} %bitcast_convert_fusion.hid_ref, s32[160,1024]{1,0:T(8,128)} %dynamic-slice_bitcast_fusion.sgn_ref, bf16[5120,256]{1,0:T(8,128)(2,1)} %bitcast.9), custom_call_target="tpu_custom_call" | custom-call | tf_op jit(solution)/shard_map/pallas_call | solution.py:222
  158.9 37.4 %shard_map.56 = f32[1024,8192]{1,0:T(8,128)} custom-call(f32[5120,1024]{1,0:T(8,128)} %shard_map.55.y_ref, bf16[256,256]{1,0:T(8,128)(2,1)} %constant.14.clone.hc_ref, bf16[256,256]{1,0:T(8,128)(2,1)} %constant.15.clone.hr_ref), custom_call_target="tpu_custom_call" | custom-call | tf_op jit(solution)/shard_map/pallas_call | solution.py:292
Async XLA Ops:
  0.0 1.3 copy-start

commit v3 on v2

--- a/solution.py
+++ b/solution.py
@@ -59,7 +59,7 @@
 
 
 def gather_kernel(
-    n, hid_ref, sgn_ref, cot_ref, y_out, hid, sgn, hb, y,
+    n, own_ref, sgn_ref, cot_ref, y_out, hid, sgn, hb, cot_t, y,
     hid_send, hid_recv, sgn_send, sgn_recv, mate_send, mate_recv, out_sem,
 ):
     toks, rows = hb.shape
@@ -90,7 +90,7 @@
 
     def send_hid(side, d):
         at = part(side, d, toks)
-        src = hid_ref.at[at] if d == 1 else hid.at[slot(side, d - 1), at]
+        src = hid.at[slot(side, d - 1), at]
         return pltpu.make_async_remote_copy(
             src_ref=src,
             dst_ref=hid.at[slot(side, d), at],
@@ -148,7 +148,7 @@
 
             def chunk(ci, carry):
                 row = ci - h * (blocks // 2)
-                c = cot_ref[pl.ds(pl.multiple_of(ci * CB, CB), CB), :]
+                c = cot_t[pl.ds(pl.multiple_of(ci * CB, CB), CB), :]
                 for f in range(0, rows, ft):
                     g = jnp.dot(c, hb[:, f : f + ft], preferred_element_type=jnp.float32)
                     for w in range(per_block):
@@ -175,14 +175,22 @@
 
     for side in range(2):
         go(send_sgn(side, 1))
+    hid[0] = own_ref[...].astype(jnp.float32)
     for side in range(2):
         go(send_hid(side, 1))
     go(mate_copies[0])
     own = pltpu.make_async_copy(sgn_ref, sgn.at[0, core], out_sem.at[0])
     own.start()
+
+    def turn(ci, carry):
+        at = pl.ds(pl.multiple_of(ci * CB, CB), CB)
+        cot_t[at, :] = cot_ref[:, at].T
+        return carry
+
+    lax.fori_loop(0, blocks, turn, 0)
     own.wait()
     wait_mate(0)
-    accumulate(hid_ref, 0, me, first=True)
+    accumulate(hid.at[0], 0, me, first=True)
 
     for d in range(1, far + 1):
         for side in range(2):
@@ -212,9 +220,9 @@
         store_block(ci).wait()
 
 
-def gathered_gradient(n, hid, sgn, cot_t):
+def gathered_gradient(n, hid, sgn, cot):
     toks, rows = hid.shape
-    width = cot_t.shape[0]
+    width = cot.shape[1]
     half = sgn.shape[0]
     far = n // 2
     vmem = pl.BlockSpec(memory_space=pltpu.VMEM)
@@ -228,6 +236,7 @@
             pltpu.VMEM((n, toks, rows), jnp.float32),
             pltpu.VMEM((n, 2, half, rows), jnp.int32),
             pltpu.VMEM((toks, rows), jnp.bfloat16),
+            pltpu.VMEM((width, toks), jnp.bfloat16),
             pltpu.VMEM((width, rows), jnp.float32),
             dma((2, far + 1)),
             dma((2, far + 1)),
@@ -240,7 +249,7 @@
         compiler_params=pltpu.CompilerParams(
             collective_id=0, has_side_effects=True, vmem_limit_bytes=60 * 1024 * 1024
         ),
-    )(hid, sgn, cot_t)
+    )(hid, sgn, cot)
 
 
 def transform_kernel(y_ref, hc_ref, hr_ref, out_ref, z):
@@ -307,7 +316,7 @@
 def body(n, hidden, cotangent, signs):
     half = signs.shape[1] // 2
     sgn = lax.dynamic_slice_in_dim(signs, lax.axis_index("ex") * half, half, axis=1).T
-    y = gathered_gradient(n, hidden[0].astype(jnp.float32), sgn, cotangent[0].T)
+    y = gathered_gradient(n, hidden[0], sgn, cotangent[0])
     return transform(n, y)[None]
 
 

time: 199 us -> 192 us (0.965)
  local copies, waits for them, and re-layouts: 6.61 us -> 2.2 us
  other arithmetic: 2.13 us -> 0 us
    unnamed x3 -> x2, local copies, waits for them, and re-layouts: 5.69 us -> 1.32 us
    convert_element_type x1 -> x0, other arithmetic: 2.13 us -> none  [body(): y = gathered_gradient(n, hidden[0].astype(jnp.float32), sgn, cotangent[0].T)]
where the time goes in v3:
time: 192 us; the launch traced here: 190 us
  Pallas kernels  187 us (97%)
  local copies, waits for them, and re-layouts  2.2 us (1%)
    pallas_call x1, Pallas kernels, gathered_gradient(): pl.pallas_call(functools.partial(gather_kernel, n), out_shape=jax.ShapeDt...  150 us
    pallas_call x1, Pallas kernels, transform(): pl.pallas_call(transform_kernel, grid=(blocks + rows // OUT_ROWS,), out_s...  37.4 us

profile of v3, /device:TPU:0, one launch (start us, length us, event | category | flops | bytes accessed | tf_op | source)
XLA Modules:
  0.0 189.5 jit_solution(17104012558052099078)
XLA Ops:
  0.0 0.0 copy-start
  0.0 1.3 copy-done
  1.3 0.9 dynamic-slice_bitcast_fusion.sgn_ref
  2.2 150.0 %shard_map.55.y_ref = f32[5120,1024]{1,0:T(8,128)} custom-call(bf16[256,1024]{1,0:T(8,128)(2,1)} %bitcast.6, s32[160,1024]{1,0:T(8,128)} %dynamic-slice_bitcast_fusion.sgn_ref, bf16[256,5120]{1,0:T(8,128)(2,1)} %bitcast.5), custom_call_target="tpu_custom_call" | custom-call | tf_op jit(solution)/shard_map/pallas_call | solution.py:230
  152.2 37.4 %shard_map.56 = f32[1024,8192]{1,0:T(8,128)} custom-call(f32[5120,1024]{1,0:T(8,128)} %shard_map.55.y_ref, bf16[256,256]{1,0:T(8,128)(2,1)} %constant.14.clone.hc_ref, bf16[256,256]{1,0:T(8,128)(2,1)} %constant.15.clone.hr_ref), custom_call_target="tpu_custom_call" | custom-call | tf_op jit(solution)/shard_map/pallas_call | solution.py:301
Async XLA Ops:
  0.0 1.3 copy-start
